TPU v7x, 32 devices: a whole 2x2x4 slice. The times are simulated.
32 devices in a mesh: expert: 2 (over x), dp: 16 (over z, y, core).
Axes of the slice: x: 2, y: 2, z: 4, core: 2. Of those that a mesh axis runs over, the one named last changes fastest.
Arguments:
- tokens: bfloat16 [384, 4096], P('expert'), may hold values from -6 to 6
- grad_out: bfloat16 [384, 4096], P('expert'), may hold values from -3 to 3
- gate_probs: bfloat16 [384, 2], P('expert'), may hold values from 0.19921875 to 1
- expert_ids: int32 [384, 2], P('expert'), may hold values from 0 to 3, all different within a row; in each aligned block of 192 rows (0 to 191, 192 to 383, ...) at most 144 rows name the same one
- capacity: int32 [4], replicated, may hold values from 72 to 144, as said below
- w_gate: bfloat16 [4096, 57344], P(None, 'dp'), may hold values from -0.09375 to 0.09375
- w_up: bfloat16 [4096, 57344], P(None, 'dp'), may hold values from -0.09375 to 0.09375
- w_down: bfloat16 [4096, 57344], P(None, 'dp'), may hold values from -0.046875 to 0.046875
Outputs:
- grad_tokens: bfloat16 [384, 4096], P('expert', 'dp')
- grad_probs: bfloat16 [384, 2], P('expert')
- grad_gate: bfloat16 [4096, 57344], P('expert', 'dp')
- grad_up: bfloat16 [4096, 57344], P('expert', 'dp')
- grad_down: bfloat16 [4096, 57344], P('expert', 'dp')
Inputs may be any that keep to these rules, and one draw needn't show every extreme that they name: `expert_ids`: the two experts of a token differ. Among the 192 tokens of one group no expert is named more than 144 times, a bound that some block reaches. Some expert has capacity 144 and another one 144 // 2.
All inputs are finite; a program needn't handle non-finite values.
Results may differ from a plain program's by a relative error of at most 0.013.
Values may be sent and summed in bfloat16 or wider, within the bound.
No kernel may reach another device: no remote copies, remote signals or barrier semaphores. Data moves between devices by JAX's collectives and lax.ppermute only.
A program may use at most 256 MiB of HBM per device.

v0:
```python
import functools

import jax
import jax.numpy as jnp
from jax import lax
from jax.experimental import pallas as pl
from jax.experimental.pallas import tpu as pltpu
from jax.sharding import PartitionSpec as P

EXPERTS = 4
CAP = 144
SHORT = 256
EXTRA = 16
BF = jnp.bfloat16
F32 = jnp.float32
MIB = 1024 * 1024

FIRST = (((0,), (0,)), ((), ()))
LAST = (((1,), (1,)), ((), ()))


def dot(a, b):
    return jnp.dot(a, b, preferred_element_type=F32)


def dotg(a, b, dims):
    return lax.dot_general(a, b, dims, preferred_element_type=F32)


def whole(shape):
    return pl.BlockSpec(shape, lambda *_: (0,) * len(shape), pipeline_mode=pl.Buffered(1))


def params(mib=60):
    return pltpu.CompilerParams(vmem_limit_bytes=mib * MIB)


def whole_smem():
    return pl.BlockSpec(memory_space=pltpu.SMEM)


def in_place():
    return pl.BlockSpec(memory_space=pl.ANY)


def my_place(shares):
    index = lax.axis_index("dp")
    return index // (shares // EXPERTS), index % 2, lax.axis_index("expert")


def pack_body(shares, ids_ref, probs_ref, tok_hbm, out_hbm, routes_ref, send_ref, sem):
    _, parity, _ = my_place(shares)
    count = tok_hbm.shape[0]
    top = send_ref.at[:count]

    @pl.when(parity == 0)
    def _():
        pltpu.make_async_copy(tok_hbm, top, sem).start()

    @pl.when(parity == 1)
    def _():
        pltpu.make_async_copy(out_hbm, top, sem).start()

    ids = ids_ref[...].astype(F32)
    routes = jnp.concatenate([ids, probs_ref[...].astype(F32), jnp.zeros((EXTRA - 4, count), F32)], axis=0).astype(BF)
    routes_ref[...] = routes
    send_ref[count:, :] = jnp.zeros((EXTRA, send_ref.shape[1]), BF)
    send_ref[count:, :count] = routes
    pltpu.make_async_copy(tok_hbm, top, sem).wait()


def pack(ids, probs, tokens, grad_out, shares):
    count, width = tokens.shape
    return pl.pallas_call(
        functools.partial(pack_body, shares),
        in_specs=[whole(ids.shape), whole(probs.shape), in_place(), in_place()],
        out_specs=[whole((EXTRA, count)), whole((count + EXTRA, width))],
        out_shape=[jax.ShapeDtypeStruct((EXTRA, count), BF), jax.ShapeDtypeStruct((count + EXTRA, width), BF)],
        scratch_shapes=[pltpu.SemaphoreType.DMA(())],
        compiler_params=params(16),
        cost_estimate=pl.CostEstimate(flops=0, bytes_accessed=4 * count * width, transcendentals=0),
        name="pack",
    )(ids, probs, tokens, grad_out)


def slot_table(routes, owner, limit, backwards):
    count = routes.shape[1]
    hit = (routes[:2] == owner.astype(F32)).astype(F32)
    named = jnp.sum(hit, axis=0, keepdims=True)
    weight = jnp.sum(hit * routes[2:4], axis=0, keepdims=True)
    row = lax.broadcasted_iota(jnp.int32, (count, count), 0)
    col = lax.broadcasted_iota(jnp.int32, (count, count), 1)
    earlier = (row < col).astype(F32).astype(BF)
    wide = jnp.broadcast_to(named, (16, count)).astype(BF)
    rank = dot(wide, earlier)[:1].astype(jnp.int32)
    kept = (named > 0) & (rank < limit)
    slot = lax.broadcasted_iota(jnp.int32, (CAP, count), 0)
    slot = jnp.where(backwards, CAP - 1 - slot, slot)
    table = ((slot == rank) & kept).astype(F32)
    return table, jnp.sum(table * weight, axis=1, keepdims=True)


class Stream:
    def __init__(self, sources, slots, sems, block, steps):
        self.sources, self.slots, self.sems, self.block = sources, slots, sems, block
        self.steps, self.whole = steps, sources[0].shape[1] == block

    def copy(self, i, step):
        source = self.sources[i]
        if not self.whole:
            source = source.at[:, pl.ds(pl.multiple_of(step * self.block, self.block), self.block)]
        slot = lax.rem(step, 2)
        return pltpu.make_async_copy(source, self.slots[i].at[slot], self.sems.at[i, slot])

    def first(self):
        for i in range(len(self.sources)):
            self.copy(i, 0).start()

    def ahead(self, step):
        @pl.when(step + 1 < self.steps)
        def _():
            for i in range(len(self.sources)):
                self.copy(i, step + 1).start()

    def wait(self, i, step):
        self.copy(i, step).wait()
        return self.slots[i].at[lax.rem(step, 2)]


def derivatives(x_ref, u_ref, p, stream, step):
    x = x_ref[...]
    wg = stream.wait(0, step)
    pre_gate = dot(x, wg[...])
    wu = stream.wait(1, step)
    pre_up = dot(x, wu[...])
    wd = stream.wait(2, step)
    back = dot(u_ref[...], wd[...])
    s = jax.nn.sigmoid(pre_gate)
    activated = pre_gate * s
    hidden = (activated * pre_up).astype(BF)
    scaled_back = p * back
    d_gate = (scaled_back * pre_up * s * (1.0 + pre_gate * (1.0 - s))).astype(BF)
    d_up = (scaled_back * activated).astype(BF)
    return d_gate, d_up, hidden, back, wg, wu


def pieces_of(total, size):
    return [(a, min(size, total - a)) for a in range(0, total, size)]


def own_body(packed, early, groups, cap_ref, routes_ref, tok_hbm, out_hbm, wg_hbm, wu_hbm, wd_hbm, *refs):
    acts_refs, refs = (refs[:3], refs[3:]) if early is None else (refs[:4], refs[4:])
    (part_hbm, prob_ref, xq_hbm, sq_hbm, filled_ref, part_ref, xq_ref, sq_ref, tok_ref, out_ref, x_ref, u_ref, p_ref,
     table_ref, acc_ref, wg_ref, wu_ref, wd_ref, sems, row_sems, out_sems) = refs
    step = pl.program_id(0)
    width, block = wg_ref.shape[1:]
    quarter = xq_ref.shape[1]
    stream = Stream((wg_hbm, wu_hbm, wd_hbm), (wg_ref, wu_ref, wd_ref), sems, block, wg_hbm.shape[1] // block)
    owner, _, group = my_place(part_ref.shape[0])
    half = part_ref.shape[0] // 2
    halves = [pltpu.make_async_copy(part_ref.at[k * half:(k + 1) * half], part_hbm.at[k * half:(k + 1) * half],
                                    out_sems.at[k]) for k in range(2)]
    shares_out = [pltpu.make_async_copy(xq_ref, xq_hbm, out_sems.at[2]),
                  pltpu.make_async_copy(sq_ref, sq_hbm, out_sems.at[3])]

    @pl.when(step == 0)
    def _():
        rows = [pltpu.make_async_copy(tok_hbm, tok_ref, row_sems.at[0]),
                pltpu.make_async_copy(out_hbm, out_ref, row_sems.at[1])]
        rows[0].start()
        stream.copy(0, 0).start()
        rows[1].start()
        stream.copy(1, 0).start()
        stream.copy(2, 0).start()
        table, p = slot_table(routes_ref[...].astype(F32), owner, cap_ref[owner], (group == 1) & (groups == 2))
        table_ref[...] = table.astype(BF)
        p_ref[...] = p
        filled_ref[...] = jnp.sum(table, axis=1, keepdims=True)
        acc_ref[...] = jnp.zeros_like(acc_ref)
        prob_ref[...] = jnp.zeros_like(prob_ref)
        rows[0].wait()
        x_ref[...] = dot(table_ref[...], tok_ref[...]).astype(BF)
        rows[1].wait()
        u_ref[...] = dot(table_ref[...], out_ref[...]).astype(BF)
        at = pl.ds(pl.multiple_of(group * quarter, quarter), quarter)
        xq_ref[...] = x_ref[:, at]
        sq_ref[...] = (p * u_ref[:, at].astype(F32)).astype(BF)
        for copy in shares_out:
            copy.start()

    stream.ahead(step)
    d_gate, d_up, hidden, back, wg, wu = derivatives(x_ref, u_ref, p_ref[...], stream, step)
    acts = (d_gate, d_up, hidden)

    def store_early():
        for ref, value in zip(acts_refs, acts):
            ref[...] = value

    if early is None:
        store_early()
    else:
        pl.when(step < early)(store_early)

        @pl.when(step >= early)
        def _():
            for i, value in enumerate(acts):
                acts_refs[3][i] = value

    prob_ref[...] += jnp.sum(hidden.astype(F32) * back, axis=1, keepdims=True)
    gate_t = d_gate.T
    up_t = d_up.T
    for a, n in pieces_of(width, 512):
        at = slice(a, a + n)
        acc_ref[at, :] += dot(wg[at, :], gate_t) + dot(wu[at, :], up_t)

    @pl.when(step == pl.num_programs(0) - 1)
    def _():
        table = table_ref[...]
        count = table.shape[1]
        shares, _, fw = part_ref.shape
        by_slot = (((0,), (1,)), ((), ()))
        if packed:
            total = prob_ref[...]
            high = total.astype(BF).astype(F32)
            lane = lax.broadcasted_iota(jnp.int32, (CAP, 128), 1)
            both = jnp.where(lane == 0, high, jnp.where(lane == 1, total - high, 0.0)).astype(BF)
            by_token = dotg(both, table, FIRST)[:EXTRA].astype(BF)
        for j in range(shares):
            part_ref[j, :count, :] = dotg(table, acc_ref[j * fw:(j + 1) * fw, :].astype(BF), by_slot).astype(BF)
            if packed:
                part_ref[j, count:, :] = jnp.zeros((EXTRA, fw), BF)
                part_ref[j, count:, :count] = by_token
            if (j + 1) % half == 0:
                halves[j // half].start()
        for copy in halves + shares_out:
            copy.wait()


def weight_slots(width, block):
    return [pltpu.VMEM((2, width, block), BF)] * 3 + [pltpu.SemaphoreType.DMA((3, 2))]


def own_group(capacity, routes, tokens, grad_out, wg, wu, wd, shares, groups, packed, block, early):
    count, width = tokens.shape
    hidden = wg.shape[1]
    steps = hidden // block
    tall = count + (EXTRA if packed else 0)
    fw = width // shares
    quarter = width // groups
    act_specs = [pl.BlockSpec((CAP, block), lambda j: (0, jnp.minimum(j, early - 1)))] * 3
    acts = [jax.ShapeDtypeStruct((CAP, early * block), BF)] * 3
    if early < steps:
        act_specs.append(pl.BlockSpec((3, CAP, block), lambda j: (0, 0, jnp.maximum(j - early, 0))))
        acts.append(jax.ShapeDtypeStruct((3, CAP, (steps - early) * block), BF))
    column = jax.ShapeDtypeStruct((CAP, 1), F32)
    share = jax.ShapeDtypeStruct((CAP, quarter), BF)
    part = jax.ShapeDtypeStruct((shares, tall, fw), BF)
    rows = pltpu.VMEM((CAP, width), BF)
    tall_rows = pltpu.VMEM((count, width), BF)
    return pl.pallas_call(
        functools.partial(own_body, packed, early if early < steps else None, groups),
        grid=(steps,),
        in_specs=[whole_smem(), whole(routes.shape)] + [in_place()] * 5,
        out_specs=act_specs + [in_place(), whole(column.shape), in_place(), in_place(), whole(column.shape)],
        out_shape=acts + [part, column, share, share, column],
        scratch_shapes=[pltpu.VMEM(part.shape, BF)] + [pltpu.VMEM(share.shape, BF)] * 2 + [tall_rows, tall_rows, rows, rows, pltpu.VMEM((CAP, 1), F32), pltpu.VMEM((CAP, count), BF),
                        pltpu.VMEM((width, CAP), F32)] + weight_slots(width, block)
        + [pltpu.SemaphoreType.DMA((2,)), pltpu.SemaphoreType.DMA((4,))],
        compiler_params=params(46),
        cost_estimate=pl.CostEstimate(
            flops=10 * CAP * width * hidden, bytes_accessed=6 * width * hidden, transcendentals=CAP * hidden),
        name="own_group",
    )(capacity, routes, tokens, grad_out, wg, wu, wd)


def joined(mine, other):
    return jnp.concatenate([mine, other], axis=0)


def merged(group, mine, other):
    first, last = jnp.where(group == 0, mine, other), jnp.where(group == 0, other, mine)
    lead = SHORT - CAP
    shared = CAP - lead
    return jnp.concatenate([first[:lead], first[lead:] + last[:shared], last[shared:]], axis=0)


def store_grads(groups, group, fits_ref, xs_ref, ss_ref, mine, other, out_refs):
    def grads(join, rows):
        for i, (rows_ref, out_ref) in enumerate(zip((xs_ref, xs_ref, ss_ref), out_refs)):
            out_ref[...] = dotg(rows_ref[:rows, :], join(mine(i), other(i)), FIRST).astype(BF)

    if groups == 2:
        @pl.when(fits_ref[0] == 1)
        def _():
            grads(functools.partial(merged, group), SHORT)

    @pl.when(fits_ref[0] == 0)
    def _():
        grads(joined, xs_ref.shape[0])


def again_body(groups, shares, steps, cap_ref, xq_ref, sq_ref, filled_ref, one_hbm, two_hbm, dg_ref, du_ref, h_ref,
               wg_hbm, wu_hbm, wd_hbm, gg_ref, gu_ref, gd_ref, xs_hbm, ss_hbm, fits_ref,
               xs_ref, ss_ref, one_ref, two_ref, xo_ref, uo_ref, po_ref, wg_ref, wu_ref, wd_ref, sems, row_sems):
    step = pl.program_id(0)
    owner, parity, group = my_place(shares)
    quarter = xs_ref.shape[1]
    count = one_ref.shape[1] - EXTRA
    stream = Stream((wg_hbm, wu_hbm, wd_hbm), (wg_ref, wu_ref, wd_ref), sems, wg_ref.shape[2], steps)
    joint = [pltpu.make_async_copy(xs_ref, xs_hbm, row_sems.at[2]), pltpu.make_async_copy(ss_ref, ss_hbm, row_sems.at[3])]

    @pl.when(step == 0)
    def _():
        rows = [pltpu.make_async_copy(one_hbm, one_ref, row_sems.at[0]),
                pltpu.make_async_copy(two_hbm, two_ref, row_sems.at[1])]
        for copy in rows:
            copy.start()
        stream.first()
        for copy in rows:
            copy.wait()
        filled = jnp.sum(filled_ref[...])
        for g in range(groups - 1):
            at = slice(g * CAP, (g + 1) * CAP)
            routes = one_ref[g, count:count + EXTRA, :count].astype(F32)
            table, p = slot_table(routes, owner, cap_ref[owner], (group == 0) & (groups == 2))
            filled += jnp.sum(table)
            po_ref[at, :] = p
            table = table.astype(BF)
            from_one = dot(table, one_ref[g, :count, :]).astype(BF)
            from_two = dot(table, two_ref[g, :count, :]).astype(BF)

            @pl.when(parity == 0)
            def _():
                xo_ref[at, :] = from_one
                uo_ref[at, :] = from_two

            @pl.when(parity == 1)
            def _():
                xo_ref[at, :] = from_two
                uo_ref[at, :] = from_one

        fits = filled <= SHORT if groups == 2 else jnp.bool_(False)
        fits_ref[0] = fits.astype(jnp.int32)
        part = pl.ds(pl.multiple_of(group * quarter, quarter), quarter)
        mine, scaled = xq_ref[...], sq_ref[...]
        other = xo_ref[:, part]
        scaled_other = (po_ref[...] * uo_ref[:, part].astype(F32)).astype(BF)
        if groups == 2:
            @pl.when(fits)
            def _():
                xs_ref[:SHORT, :] = merged(group, mine, other)
                ss_ref[:SHORT, :] = merged(group, scaled, scaled_other)

        @pl.when(jnp.logical_not(fits))
        def _():
            xs_ref[...] = joined(mine, other)
            ss_ref[...] = joined(scaled, scaled_other)

        for copy in joint:
            copy.start()

    stream.ahead(step)
    acts = derivatives(xo_ref, uo_ref, po_ref[...], stream, step)
    own = (dg_ref, du_ref, h_ref)
    store_grads(groups, group, fits_ref, xs_ref, ss_ref, lambda i: own[i][...], lambda i: acts[i], (gg_ref, gu_ref, gd_ref))

    @pl.when(step == steps - 1)
    def _():
        for copy in joint:
            copy.wait()


def grads_again(capacity, xq, sq, filled, one, two, dg, du, h, wg, wu, wd, groups, shares, block):
    width, hidden = wg.shape
    others = (groups - 1) * CAP
    quarter = width // groups
    steps = dg.shape[1] // block
    act = pl.BlockSpec((CAP, block), lambda j: (0, j))
    grad = pl.BlockSpec((quarter, block), lambda j: (0, j))
    arrived = pltpu.VMEM(one.shape, BF)
    rows = pltpu.VMEM((others, width), BF)
    joint = jax.ShapeDtypeStruct((CAP + others, quarter), BF)
    return pl.pallas_call(
        functools.partial(again_body, groups, shares, steps),
        grid=(steps,),
        in_specs=[whole_smem(), whole(xq.shape), whole(sq.shape), whole(filled.shape), in_place(), in_place(),
                  act, act, act, in_place(), in_place(), in_place()],
        out_specs=[grad] * 3 + [in_place()] * 2 + [whole_smem()],
        out_shape=[jax.ShapeDtypeStruct((quarter, hidden), BF)] * 3 + [joint] * 2 + [jax.ShapeDtypeStruct((1,), jnp.int32)],
        scratch_shapes=[pltpu.VMEM(joint.shape, BF)] * 2 + [arrived, arrived, rows, rows, pltpu.VMEM((others, 1), F32)]
        + weight_slots(width, block) + [pltpu.SemaphoreType.DMA((4,))],
        compiler_params=params(52 if groups == 2 else 60),
        cost_estimate=pl.CostEstimate(
            flops=(6 * others * width + 6 * (CAP + others) * quarter) * steps * block,
            bytes_accessed=6 * (width + quarter) * steps * block, transcendentals=others * steps * block),
        name="grads_again",
    )(capacity, xq, sq, filled, one, two, dg, du, h, wg, wu, wd)


def given_body(groups, shares, fits_ref, xs_ref, ss_ref, mine_ref, other_ref, gg_in, gu_in, gd_in, gg_ref, gu_ref, gd_ref):
    _, _, group = my_place(shares)
    store_grads(groups, group, fits_ref, xs_ref, ss_ref, lambda i: mine_ref[i], lambda i: other_ref[i], (gg_ref, gu_ref, gd_ref))


def grads_given(fits, xs, ss, mine, other, grads, groups, shares, block):
    quarter, hidden = grads[0].shape
    steps = mine.shape[2] // block
    early = hidden // block - steps
    grad = pl.BlockSpec((quarter, block), lambda j: (0, j + early))
    act = pl.BlockSpec((3, CAP, block), lambda j: (0, 0, j))
    return pl.pallas_call(
        functools.partial(given_body, groups, shares),
        grid=(steps,),
        in_specs=[whole_smem(), whole(xs.shape), whole(ss.shape), act, act] + [in_place()] * 3,
        out_specs=[grad] * 3,
        out_shape=[jax.ShapeDtypeStruct((quarter, hidden), BF)] * 3,
        input_output_aliases={5: 0, 6: 1, 7: 2},
        compiler_params=params(24),
        cost_estimate=pl.CostEstimate(
            flops=6 * xs.shape[0] * quarter * steps * block, bytes_accessed=6 * quarter * steps * block, transcendentals=0),
        name="grads_given",
    )(fits, xs, ss, mine, other, *grads)


def block_of(hidden, largest):
    for size in (512, 256, 128):
        if size <= largest and hidden % size == 0:
            return size
    return hidden


def per_device(tokens, grad_out, gate_probs, expert_ids, capacity, w_gate, w_up, w_down):
    groups = lax.axis_size("expert")
    shares = lax.axis_size("dp")
    count, width = tokens.shape
    hidden = w_gate.shape[1]
    per_expert = shares // EXPERTS
    packed = width // shares >= count
    block = block_of(hidden, 512)
    steps = hidden // block
    early = steps - steps * 3 // 7 if groups == 2 else steps

    routes, send = pack(expert_ids.T, gate_probs.T, tokens, grad_out, shares)
    arounds = [[(i, (i + shift) % groups) for i in range(groups)] for shift in range(1, groups)]
    one = [lax.ppermute(send, "expert", around) for around in arounds]

    *acts, part, prob, xq, sq, filled = own_group(
        capacity, routes, tokens, grad_out, w_gate, w_up, w_down, shares, groups, packed, block, early)

    one, part = lax.optimization_barrier((one, part))
    swap = [(i, i ^ 1) for i in range(shares)]
    two = [lax.ppermute(rows, "dp", swap) for rows in one]
    if early < steps:
        late = acts.pop()
        late_other = lax.ppermute(late, "expert", arounds[0])
    arrived = lax.all_to_all(part, "dp", split_axis=0, concat_axis=0, tiled=True)

    def stacked(parts):
        return parts[0][None] if len(parts) == 1 else jnp.stack(parts)

    *grads, xs, ss, fits = grads_again(
        capacity, xq, sq, filled, stacked(one), stacked(two), *acts, w_gate, w_up, w_down, groups, shares, block)
    if early < steps:
        grads = grads_given(fits, xs, ss, late, late_other, grads, groups, shares, block_of(late.shape[2], 256))
    grad_gate, grad_up, grad_down = grads

    token_grad = jnp.sum(arrived[:, :count].astype(F32), axis=0).astype(BF)
    if packed:
        ends = arrived[:, count:count + 2, :count].astype(F32)
        by_expert = jnp.sum(ends.reshape(EXPERTS, per_expert * 2, count), axis=1)
    else:
        owner, _, group = my_place(shares)
        table, _ = slot_table(routes.astype(F32), owner, capacity[owner], (group == 1) & (groups == 2))
        mine = jnp.sum(table * prob, axis=0)
        one_hot = (jnp.arange(EXPERTS) == owner).astype(F32)
        by_expert = lax.psum(one_hot[:, None] * mine[None, :], "dp")
    match = expert_ids[:, :, None] == jnp.arange(EXPERTS, dtype=jnp.int32)
    prob_grad = jnp.sum(jnp.where(match, by_expert.T[:, None, :], 0.0), axis=2).astype(BF)
    return (token_grad, prob_grad, grad_gate, grad_up, grad_down)


def solution(mesh):
    return jax.shard_map(
        per_device,
        mesh=mesh,
        in_specs=(
            P("expert", None),
            P("expert", None),
            P("expert", None),
            P("expert", None),
            P(),
            P(None, "dp"),
            P(None, "dp"),
            P(None, "dp"),
        ),
        out_specs=(
            P("expert", "dp"),
            P("expert", None),
            P("expert", "dp"),
            P("expert", "dp"),
            P("expert", "dp"),
        ),
        check_vma=False,
    )
```

profile of v0, /device:TPU:0, one launch (start us, length us, event | category | flops | bytes accessed | tf_op | source)
XLA Modules:
  0.0 106.0 jit_solution(6985554685557911932)
XLA Ops:
  0.6 0.0 copy-start.10
  0.6 0.0 copy-start
  0.7 1.4 %copy-done = bf16[192,4096]{1,0:T(8,128)(2,1)S(1)} copy-done((bf16[192,4096]{1,0:T(8,128)(2,1)S(1)}, bf16[192,4096]{1,0:T(8,128)(2,1)}, u32[]{:S(2)}) %copy-start) | copy-done | bytes 1572888
  2.1 0.0 copy-start.2
  2.1 1.4 %copy-done.2 = bf16[192,4096]{1,0:T(8,128)(2,1)S(1)} copy-done((bf16[192,4096]{1,0:T(8,128)(2,1)S(1)}, bf16[192,4096]{1,0:T(8,128)(2,1)}, u32[]{:S(2)}) %copy-start.2) | copy-done | bytes 1572888
  3.5 0.0 copy-start.8
  3.5 0.7 copy-done.8
  4.1 0.0 copy-start.11
  4.1 0.7 copy-done.11
  4.8 0.0 copy-start.1
  4.8 0.0 copy-start.3
  4.8 0.1 pack.1
  5.0 3.0 %collective-permute-start = (bf16[208,4096]{1,0:T(8,128)(2,1)S(1)}, bf16[208,4096]{1,0:T(8,128)(2,1)}, u32[]{:S(2)}, u32[]{:S(2)}) collective-permute-start(bf16[208,4096]{1,0:T(8,128)(2,1)S(1)} %get-tuple-element.26), channel_id=1, source_target_pairs={{0,16},{16,0},{1,17},{17,1},{2,18},{18,2},{3,19},{19,3},{4,20},{20... | collective-permute-start | bytes 5111816 | tf_op jit(solution)/shard_map/ppermute | solution.py:445
  8.0 0.0 copy-done.10
  8.0 0.0 copy-done.1
  8.0 0.0 copy-done.3
  8.0 41.0 %own_group.1 = (bf16[144,2048]{1,0:T(8,128)(2,1)S(1)}, bf16[144,2048]{1,0:T(8,128)(2,1)S(1)}, bf16[144,2048]{1,0:T(8,128)(2,1)S(1)}, bf16[3,144,1536]{2,1,0:T(8,...) custom-call(s32[4]{0:T(128)S(1)} %copy-done.10, ...), custom_call_target="tpu_custom_call" | custom-call | flops 21139292160 | bytes 88080384 | tf_op jit(solution)/shard_map/own_group/pallas_call | solution.py:260
  49.0 0.0 copy-start.6
  49.0 0.8 copy-done.6
  49.8 0.0 copy-start.7
  49.8 0.8 copy-done.7
  50.6 0.0 collective-permute-done
  50.6 0.0 collective-permute-start.1
  50.6 6.2 %all-to-all-start = ((bf16[16,208,256]{2,1,0:T(8,128)(2,1)}), bf16[16,208,256]{2,1,0:T(8,128)(2,1)}, u32[]{:S(2)}, u32[]{:S(2)}) async-start(bf16[16,208,256]{2,1,0:T(8,128)(2,1)} %get-tuple-element.29), calls=%async_computation | async-start | bytes 3407872 | tf_op jit(solution)/shard_map/all_to_all | solution.py:456
  56.9 1.5 %collective-permute-start.2 = (bf16[3,144,1536]{2,1,0:T(8,128)(2,1)S(1)}, bf16[3,144,1536]{2,1,0:T(8,128)(2,1)S(1)}, u32[]{:S(2)}, u32[]{:S(2)}) collective-permute-start(bf16[3,144,1536]{2,1,0:T(8,128)(2,1)S(1)} %get-tuple-element.40.mine_ref), channel_id=1, source_target_pairs={{0,16},{16,0},{1,17},{17,1},{2,18},{18,2},{3,19},{19,3},{4,20},{20... | collective-permute-start | bytes 3981320 | tf_op jit(solution)/shard_map/ppermute | solution.py:455
  58.4 0.0 collective-permute-done.1
  58.5 30.9 %grads_again.1 = (bf16[2048,3584]{1,0:T(8,128)(2,1)}, bf16[2048,3584]{1,0:T(8,128)(2,1)}, bf16[2048,3584]{1,0:T(8,128)(2,1)}, bf16[288,2048]{1,0:T(8,128)(2,1)}, bf16[288,2048]{1,0:T(8,128)(2,1)}, /*index=5*/s32[1]{0:T(128)}) custom-call(s32[4]{0:T(128)S(1)} %copy-done.10, bf16[144,2048]{1,0:T(8,128)(2,1)S(1)} %get-tuple-element.30.xq_ref, ...), custom_call_target="tpu_custom_call" | custom-call | flops 14495514624 | bytes 75497472 | tf_op jit(solution)/shard_map/grads_again/pallas_call | solution.py:383
  89.4 0.0 collective-permute-done.2.other_ref
  89.4 0.0 copy-start.4
  89.4 1.3 %copy-done.4 = bf16[288,2048]{1,0:T(8,128)(2,1)S(1)} copy-done((bf16[288,2048]{1,0:T(8,128)(2,1)S(1)}, bf16[288,2048]{1,0:T(8,128)(2,1)}, u32[]{:S(2)}) %copy-start.4) | copy-done | bytes 1179672
  90.6 0.0 copy-start.5
  90.6 1.3 %copy-done.5 = bf16[288,2048]{1,0:T(8,128)(2,1)S(1)} copy-done((bf16[288,2048]{1,0:T(8,128)(2,1)S(1)}, bf16[288,2048]{1,0:T(8,128)(2,1)}, u32[]{:S(2)}) %copy-start.5) | copy-done | bytes 1179672
  91.9 0.0 copy-start.9
  91.9 10.3 %grads_given.1 = (bf16[2048,3584]{1,0:T(8,128)(2,1)}, bf16[2048,3584]{1,0:T(8,128)(2,1)}, bf16[2048,3584]{1,0:T(8,128)(2,1)}) custom-call(s32[1]{0:T(128)} %get-tuple-element.37.fits_ref, bf16[288,2048]{1,0:T(8,128)(2,1)S(1)} %copy-done.4, bf16[288,2048]{1,0:T(8,128)(2,1)S(1)} %copy-done.5, ...), custom_call_target="tpu_custom_call", output_to_operand_aliasing={{0}: (5, {}), {1}: (6, {}), {2}: (7, {})} | custom-call | flops 5435817984 | bytes 18874368 | tf_op jit(solution)/shard_map/grads_given/pallas_call | solution.py:411
  102.2 0.0 all-to-all-done
  102.2 0.9 convert_reduce_fusion
  103.1 0.0 copy-done.9
  103.1 0.6 select_reduce_fusion
  103.7 2.3 %slice_reduce_fusion = bf16[192,256]{1,0:T(8,128)(2,1)} fusion(bf16[16,208,256]{2,1,0:T(8,128)(2,1)} %all-to-all-done), kind=kLoop, calls=%fused_computation | loop fusion | flops 737280 | bytes 1671168 | tf_op jit(solution)/shard_map/reduce_sum | solution.py:467
  (2 shorter events, 0.0 us)
Async XLA Ops:
  0.6 7.3 %copy-start.10 = (s32[4]{0:T(128)S(1)}, s32[4]{0:T(128)}, u32[]{:S(2)}) copy-start(s32[4]{0:T(128)} %cap_ref.3) | copy-start | bytes 52
  0.6 1.4 %copy-start = (bf16[192,4096]{1,0:T(8,128)(2,1)S(1)}, bf16[192,4096]{1,0:T(8,128)(2,1)}, u32[]{:S(2)}) copy-start(bf16[192,4096]{1,0:T(8,128)(2,1)} %tok_hbm.3) | copy-start | bytes 4718596
  2.1 1.4 %copy-start.2 = (bf16[192,4096]{1,0:T(8,128)(2,1)S(1)}, bf16[192,4096]{1,0:T(8,128)(2,1)}, u32[]{:S(2)}) copy-start(bf16[192,4096]{1,0:T(8,128)(2,1)} %out_hbm.3) | copy-start | bytes 4718596
  3.5 0.7 copy-start.8
  4.1 0.7 copy-start.11
  4.8 3.1 %copy-start.1 = (bf16[192,4096]{1,0:T(8,128)(2,1)S(1)}, bf16[192,4096]{1,0:T(8,128)(2,1)}, u32[]{:S(2)}) copy-start(bf16[192,4096]{1,0:T(8,128)(2,1)} %tok_hbm.3) | copy-start | bytes 4718596
  4.8 3.1 %copy-start.3 = (bf16[192,4096]{1,0:T(8,128)(2,1)S(1)}, bf16[192,4096]{1,0:T(8,128)(2,1)}, u32[]{:S(2)}) copy-start(bf16[192,4096]{1,0:T(8,128)(2,1)} %out_hbm.3) | copy-start | bytes 4718596
  5.0 45.7 %collective-permute-start = (bf16[208,4096]{1,0:T(8,128)(2,1)S(1)}, bf16[208,4096]{1,0:T(8,128)(2,1)}, u32[]{:S(2)}, u32[]{:S(2)}) collective-permute-start(bf16[208,4096]{1,0:T(8,128)(2,1)S(1)} %get-tuple-element.26), channel_id=1, source_target_pairs={{0,16},{16,0},{1,17},{17,1},{2,18},{18,2},{3,19},{19,3},{4,20},{20... | collective-permute-start | bytes 5111816 | tf_op jit(solution)/shard_map/ppermute | solution.py:445
  49.0 0.8 copy-start.6
  49.8 0.8 copy-start.7
  50.6 7.8 %collective-permute-start.1 = (bf16[208,4096]{1,0:T(8,128)(2,1)}, bf16[208,4096]{1,0:T(8,128)(2,1)}, u32[]{:S(2)}, u32[]{:S(2)}) collective-permute-start(bf16[208,4096]{1,0:T(8,128)(2,1)} %collective-permute-done), channel_id=1, source_target_pairs={{0,1},{1,0},{2,3},{3,2},{4,5},{5,4},{6,7},{7,6},{8,9},{9,8},{10,11... | collective-permute-start | bytes 5111816 | tf_op jit(solution)/shard_map/ppermute | solution.py:452
  50.6 51.5 %all-to-all-start = ((bf16[16,208,256]{2,1,0:T(8,128)(2,1)}), bf16[16,208,256]{2,1,0:T(8,128)(2,1)}, u32[]{:S(2)}, u32[]{:S(2)}) async-start(bf16[16,208,256]{2,1,0:T(8,128)(2,1)} %get-tuple-element.29), calls=%async_computation | async-start | bytes 3407872 | tf_op jit(solution)/shard_map/all_to_all | solution.py:456
  56.9 32.5 %collective-permute-start.2 = (bf16[3,144,1536]{2,1,0:T(8,128)(2,1)S(1)}, bf16[3,144,1536]{2,1,0:T(8,128)(2,1)S(1)}, u32[]{:S(2)}, u32[]{:S(2)}) collective-permute-start(bf16[3,144,1536]{2,1,0:T(8,128)(2,1)S(1)} %get-tuple-element.40.mine_ref), channel_id=1, source_target_pairs={{0,16},{16,0},{1,17},{17,1},{2,18},{18,2},{3,19},{19,3},{4,20},{20... | collective-permute-start | bytes 3981320 | tf_op jit(solution)/shard_map/ppermute | solution.py:455
  89.4 1.3 %copy-start.4 = (bf16[288,2048]{1,0:T(8,128)(2,1)S(1)}, bf16[288,2048]{1,0:T(8,128)(2,1)}, u32[]{:S(2)}) copy-start(bf16[288,2048]{1,0:T(8,128)(2,1)} %get-tuple-element.38.xs_ref) | copy-start | bytes 3538948
  90.6 1.3 %copy-start.5 = (bf16[288,2048]{1,0:T(8,128)(2,1)S(1)}, bf16[288,2048]{1,0:T(8,128)(2,1)}, u32[]{:S(2)}) copy-start(bf16[288,2048]{1,0:T(8,128)(2,1)} %get-tuple-element.39.ss_ref) | copy-start | bytes 3538948
  91.9 11.2 %copy-start.9 = (s32[192,2]{0,1:T(2,128)S(1)}, s32[192,2]{0,1:T(2,128)}, u32[]{:S(2)}) copy-start(s32[192,2]{0,1:T(2,128)} %param.11) | copy-start | bytes 4612
where the time goes:
time: 106 us
  Pallas kernels  82.3 us (78%)
  starting transfers between devices  10.8 us (10%)
  local copies, waits for them, and re-layouts  8.34 us (8%)
  other arithmetic  3.78 us (4%)
    pallas_call x1, Pallas kernels, own_group(): pl.pallas_call(functools.partial(own_body, packed, early if early < steps...  41 us
    pallas_call x1, Pallas kernels, grads_again(): pl.pallas_call(functools.partial(again_body, groups, shares, steps), grid...  30.9 us
    pallas_call x1, Pallas kernels, grads_given(): pl.pallas_call(functools.partial(given_body, groups, shares), grid=(steps...  10.3 us
    unnamed x24, local copies, waits for them, and re-layouts  8.33 us
    all_to_all x1, starting transfers between devices, per_device(): lax.all_to_all(part, 'dp', split_axis=0, concat_axis=0, tiled=True)  6.24 us
    ppermute x1, starting transfers between devices, per_device(): one = [lax.ppermute(send, 'expert', around) for around in arounds]  3 us
    reduce_sum x1, other arithmetic, per_device(): token_grad = jnp.sum(arrived[:, :count].astype(F32), axis=0).astype(BF)  2.29 us
  transfers between devices with their start and end apart: 4, of which 0 were waited for; matrix products, arithmetic and copies ran while one was open for 0% of the time, Pallas kernels for 78%

commit v1 on v0

--- a/solution.py
+++ b/solution.py
@@ -48,36 +48,54 @@
     return index // (shares // EXPERTS), index % 2, lax.axis_index("expert")
 
 
-def pack_body(shares, ids_ref, probs_ref, tok_hbm, out_hbm, routes_ref, send_ref, sem):
+def pack_body(shares, ids_hbm, probs_hbm, tok_hbm, out_hbm, routes_hbm, send_hbm, ids_ref, probs_ref, routes_ref, rows_ref,
+              in_sems, out_sems):
     _, parity, _ = my_place(shares)
     count = tok_hbm.shape[0]
-    top = send_ref.at[:count]
-
-    @pl.when(parity == 0)
-    def _():
-        pltpu.make_async_copy(tok_hbm, top, sem).start()
-
-    @pl.when(parity == 1)
-    def _():
-        pltpu.make_async_copy(out_hbm, top, sem).start()
-
+    half = count // 2
+    tops = [slice(0, half), slice(half, count)]
+    small = [pltpu.make_async_copy(ids_hbm, ids_ref, in_sems.at[2]), pltpu.make_async_copy(probs_hbm, probs_ref, in_sems.at[3])]
+    for copy in small:
+        copy.start()
+
+    def arrival(rows_hbm, k):
+        return pltpu.make_async_copy(rows_hbm.at[tops[k]], rows_ref.at[tops[k]], in_sems.at[k])
+
+    for value, rows_hbm in enumerate((tok_hbm, out_hbm)):
+        @pl.when(parity == value)
+        def _():
+            for k in range(2):
+                arrival(rows_hbm, k).start()
+
+    for copy in small:
+        copy.wait()
     ids = ids_ref[...].astype(F32)
     routes = jnp.concatenate([ids, probs_ref[...].astype(F32), jnp.zeros((EXTRA - 4, count), F32)], axis=0).astype(BF)
     routes_ref[...] = routes
-    send_ref[count:, :] = jnp.zeros((EXTRA, send_ref.shape[1]), BF)
-    send_ref[count:, :count] = routes
-    pltpu.make_async_copy(tok_hbm, top, sem).wait()
+    rows_ref[count:, :] = jnp.zeros((EXTRA, rows_ref.shape[1]), BF)
+    rows_ref[count:, :count] = routes
+    below = slice(count, count + EXTRA)
+    leaving = [pltpu.make_async_copy(rows_ref.at[at], send_hbm.at[at], out_sems.at[k]) for k, at in enumerate(tops + [below])]
+    leaving.append(pltpu.make_async_copy(routes_ref, routes_hbm, out_sems.at[3]))
+    leaving[2].start()
+    leaving[3].start()
+    for k in range(2):
+        arrival(tok_hbm, k).wait()
+        leaving[k].start()
+    for copy in leaving:
+        copy.wait()
 
 
 def pack(ids, probs, tokens, grad_out, shares):
     count, width = tokens.shape
     return pl.pallas_call(
         functools.partial(pack_body, shares),
-        in_specs=[whole(ids.shape), whole(probs.shape), in_place(), in_place()],
-        out_specs=[whole((EXTRA, count)), whole((count + EXTRA, width))],
+        in_specs=[in_place()] * 4,
+        out_specs=[in_place()] * 2,
         out_shape=[jax.ShapeDtypeStruct((EXTRA, count), BF), jax.ShapeDtypeStruct((count + EXTRA, width), BF)],
-        scratch_shapes=[pltpu.SemaphoreType.DMA(())],
-        compiler_params=params(16),
+        scratch_shapes=[pltpu.VMEM(ids.shape, ids.dtype), pltpu.VMEM(probs.shape, BF), pltpu.VMEM((EXTRA, count), BF),
+                        pltpu.VMEM((count + EXTRA, width), BF), pltpu.SemaphoreType.DMA((4,)), pltpu.SemaphoreType.DMA((4,))],
+        compiler_params=params(),
         cost_estimate=pl.CostEstimate(flops=0, bytes_accessed=4 * count * width, transcendentals=0),
         name="pack",
     )(ids, probs, tokens, grad_out)
@@ -248,13 +266,13 @@
     fw = width // shares
     quarter = width // groups
     act_specs = [pl.BlockSpec((CAP, block), lambda j: (0, jnp.minimum(j, early - 1)))] * 3
-    acts = [jax.ShapeDtypeStruct((CAP, early * block), BF)] * 3
+    acts = [pltpu.HBM((CAP, early * block), BF)] * 3
     if early < steps:
         act_specs.append(pl.BlockSpec((3, CAP, block), lambda j: (0, 0, jnp.maximum(j - early, 0))))
-        acts.append(jax.ShapeDtypeStruct((3, CAP, (steps - early) * block), BF))
-    column = jax.ShapeDtypeStruct((CAP, 1), F32)
-    share = jax.ShapeDtypeStruct((CAP, quarter), BF)
-    part = jax.ShapeDtypeStruct((shares, tall, fw), BF)
+        acts.append(pltpu.HBM((3, CAP, (steps - early) * block), BF))
+    column = pltpu.HBM((CAP, 1), F32)
+    share = pltpu.HBM((CAP, quarter), BF)
+    part = pltpu.HBM((shares, tall, fw), BF)
     rows = pltpu.VMEM((CAP, width), BF)
     tall_rows = pltpu.VMEM((count, width), BF)
     return pl.pallas_call(
@@ -270,7 +288,7 @@
         cost_estimate=pl.CostEstimate(
             flops=10 * CAP * width * hidden, bytes_accessed=6 * width * hidden, transcendentals=CAP * hidden),
         name="own_group",
-    )(capacity, routes, tokens, grad_out, wg, wu, wd)
+    )(capacity, pltpu.with_memory_space_constraint(routes, pltpu.HBM), tokens, grad_out, wg, wu, wd)
 
 
 def joined(mine, other):
@@ -389,7 +407,7 @@
         out_shape=[jax.ShapeDtypeStruct((quarter, hidden), BF)] * 3 + [joint] * 2 + [jax.ShapeDtypeStruct((1,), jnp.int32)],
         scratch_shapes=[pltpu.VMEM(joint.shape, BF)] * 2 + [arrived, arrived, rows, rows, pltpu.VMEM((others, 1), F32)]
         + weight_slots(width, block) + [pltpu.SemaphoreType.DMA((4,))],
-        compiler_params=params(52 if groups == 2 else 60),
+        compiler_params=params(),
         cost_estimate=pl.CostEstimate(
             flops=(6 * others * width + 6 * (CAP + others) * quarter) * steps * block,
             bytes_accessed=6 * (width + quarter) * steps * block, transcendentals=others * steps * block),
@@ -415,7 +433,7 @@
         out_specs=[grad] * 3,
         out_shape=[jax.ShapeDtypeStruct((quarter, hidden), BF)] * 3,
         input_output_aliases={5: 0, 6: 1, 7: 2},
-        compiler_params=params(24),
+        compiler_params=params(),
         cost_estimate=pl.CostEstimate(
             flops=6 * xs.shape[0] * quarter * steps * block, bytes_accessed=6 * quarter * steps * block, transcendentals=0),
         name="grads_given",
@@ -461,7 +479,7 @@
     *grads, xs, ss, fits = grads_again(
         capacity, xq, sq, filled, stacked(one), stacked(two), *acts, w_gate, w_up, w_down, groups, shares, block)
     if early < steps:
-        grads = grads_given(fits, xs, ss, late, late_other, grads, groups, shares, block_of(late.shape[2], 256))
+        grads = grads_given(fits, xs, ss, late, late_other, grads, groups, shares, block)
     grad_gate, grad_up, grad_down = grads
 
     token_grad = jnp.sum(arrived[:, :count].astype(F32), axis=0).astype(BF)

time: 106 us -> 101 us (0.953)
  local copies, waits for them, and re-layouts: 8.34 us -> 1.27 us
  Pallas kernels: 82.3 us -> 87.7 us
  other arithmetic: 3.78 us -> 1.51 us
  starting transfers between devices: 10.8 us -> 9.71 us
    unnamed x24 -> x10, local copies, waits for them, and re-layouts: 8.33 us -> 1.26 us
    pallas_call x1, Pallas kernels: 0.13 us -> 2.53 us  [pack(): pl.pallas_call(functools.partial(pack_body, shares), in_specs=[in_place()...]
    pallas_call x1, Pallas kernels: 10.3 us -> 11.8 us  [grads_given(): pl.pallas_call(functools.partial(given_body, groups, shares), grid=(steps...]
    reduce_sum x1, other arithmetic: 2.29 us -> 0.86 us  [per_device(): token_grad = jnp.sum(arrived[:, :count].astype(F32), axis=0).astype(BF)]
  transfers between devices with their start and end apart: 4 -> 4, of which waited for: 0 -> 0; matrix products, arithmetic and copies ran while one was open for 0% -> 0% of each run, Pallas kernels for 78% -> 84%
where the time goes in v1:
time: 101 us
  Pallas kernels  87.7 us (87%)
  starting transfers between devices  9.71 us (10%)
  other arithmetic  1.51 us (1%)
  local copies, waits for them, and re-layouts  1.27 us (1%)
    pallas_call x1, Pallas kernels, own_group(): pl.pallas_call(functools.partial(own_body, packed, early if early < steps...  41.9 us
    pallas_call x1, Pallas kernels, grads_again(): pl.pallas_call(functools.partial(again_body, groups, shares, steps), grid...  31.5 us
    pallas_call x1, Pallas kernels, grads_given(): pl.pallas_call(functools.partial(given_body, groups, shares), grid=(steps...  11.8 us
    all_to_all x1, starting transfers between devices, per_device(): lax.all_to_all(part, 'dp', split_axis=0, concat_axis=0, tiled=True)  6.06 us
    ppermute x1, starting transfers between devices, per_device(): one = [lax.ppermute(send, 'expert', around) for around in arounds]  3 us
    pallas_call x1, Pallas kernels, pack(): pl.pallas_call(functools.partial(pack_body, shares), in_specs=[in_place()...  2.53 us
  transfers between devices with their start and end apart: 4, of which 0 were waited for; matrix products, arithmetic and copies ran while one was open for 0% of the time, Pallas kernels for 84%

profile of v1, /device:TPU:0, one launch (start us, length us, event | category | flops | bytes accessed | tf_op | source)
XLA Modules:
  0.0 101.0 jit_solution(13205057492923684307)
XLA Ops:
  0.6 0.0 copy-start.1
  0.6 0.0 copy-start
  0.7 0.0 copy-start.2
  0.7 2.5 %pack.1 = (bf16[16,192]{1,0:T(8,128)(2,1)}, bf16[208,4096]{1,0:T(8,128)(2,1)}) custom-call(s32[2,192]{1,0:T(2,128)} %bitcast.7, bf16[2,192]{1,0:T(2,128)(2,1)} %bitcast.8, bf16[192,4096]{1,0:T(8,128)(2,1)} %tok_hbm.3, bf16[192,4096]{1,0:T(8,128)(2,1)} %out_hbm.3), custom_call_target="tpu_custom_call" | custom-call | bytes 3145728 | tf_op jit(solution)/shard_map/pack/pallas_call | solution.py:91
  3.2 3.0 %collective-permute-start = (bf16[208,4096]{1,0:T(8,128)(2,1)}, bf16[208,4096]{1,0:T(8,128)(2,1)}, u32[]{:S(2)}, u32[]{:S(2)}) collective-permute-start(bf16[208,4096]{1,0:T(8,128)(2,1)} %get-tuple-element.26), channel_id=1, source_target_pairs={{0,16},{16,0},{1,17},{17,1},{2,18},{18,2},{3,19},{19,3},{4,20},{20... | collective-permute-start | bytes 5111816 | tf_op jit(solution)/shard_map/ppermute | solution.py:463
  6.2 0.0 copy-done.1
  6.2 0.0 copy-done
  6.2 0.0 copy-done.2
  6.2 41.9 %own_group.1 = (bf16[144,2048]{1,0:T(8,128)(2,1)}, bf16[144,2048]{1,0:T(8,128)(2,1)}, bf16[144,2048]{1,0:T(8,128)(2,1)}, bf16[3,144,1536]{2,1,0:T(8,128)(2,1)}, ...) custom-call(s32[4]{0:T(128)S(1)} %copy-done.2, ...), custom_call_target="tpu_custom_call" | custom-call | flops 21139292160 | bytes 88080384 | tf_op jit(solution)/shard_map/own_group/pallas_call | solution.py:278
  48.1 0.0 collective-permute-done
  48.1 0.1 collective-permute-start.1
  48.2 6.1 %all-to-all-start = ((bf16[16,208,256]{2,1,0:T(8,128)(2,1)}), bf16[16,208,256]{2,1,0:T(8,128)(2,1)S(1)}, u32[]{:S(2)}, u32[]{:S(2)}) async-start(bf16[16,208,256]{2,1,0:T(8,128)(2,1)} %get-tuple-element.29), calls=%async_computation | async-start | bytes 3407872 | tf_op jit(solution)/shard_map/all_to_all | solution.py:474
  54.3 0.6 collective-permute-start.2
  54.8 0.0 collective-permute-done.1
  54.8 0.0 copy-start.3
  54.8 1.2 %copy-done.3 = bf16[208,4096]{1,0:T(8,128)(2,1)} copy-done((bf16[208,4096]{1,0:T(8,128)(2,1)}, bf16[208,4096]{1,0:T(8,128)(2,1)S(1)}, u32[]{:S(2)}) %copy-start.3) | copy-done | bytes 1703960
  56.1 31.5 %grads_again.1 = (bf16[2048,3584]{1,0:T(8,128)(2,1)}, bf16[2048,3584]{1,0:T(8,128)(2,1)}, bf16[2048,3584]{1,0:T(8,128)(2,1)}, bf16[288,2048]{1,0:T(8,128)(2,1)}, bf16[288,2048]{1,0:T(8,128)(2,1)}, /*index=5*/s32[1]{0:T(128)}) custom-call(s32[4]{0:T(128)} %cap_ref.3, bf16[144,2048]{1,0:T(8,128)(2,1)} %get-tuple-element.30.xq_ref, ...), custom_call_target="tpu_custom_call" | custom-call | flops 14495514624 | bytes 75497472 | tf_op jit(solution)/shard_map/grads_again/pallas_call | solution.py:401
  87.6 0.0 collective-permute-done.2.other_ref
  87.6 0.0 copy-start.4
  87.6 11.8 %grads_given.1 = (bf16[2048,3584]{1,0:T(8,128)(2,1)}, bf16[2048,3584]{1,0:T(8,128)(2,1)}, bf16[2048,3584]{1,0:T(8,128)(2,1)}) custom-call(s32[1]{0:T(128)} %get-tuple-element.37.fits_ref, bf16[288,2048]{1,0:T(8,128)(2,1)} %get-tuple-element.38.xs_ref, ...), custom_call_target="tpu_custom_call", output_to_operand_aliasing={{0}: (5, {}), {1}: (6, {}), {2}: (7, {})} | custom-call | flops 5435817984 | bytes 18874368 | tf_op jit(solution)/shard_map/grads_given/pallas_call | solution.py:429
  99.4 0.0 all-to-all-done
  99.5 0.0 copy-done.4
  99.5 0.6 select_reduce_fusion
  100.1 0.9 slice_reduce_fusion
  (3 shorter events, 0.1 us)
Async XLA Ops:
  0.6 5.6 %copy-start.1 = (bf16[192,4096]{1,0:T(8,128)(2,1)S(1)}, bf16[192,4096]{1,0:T(8,128)(2,1)}, u32[]{:S(2)}) copy-start(bf16[192,4096]{1,0:T(8,128)(2,1)} %out_hbm.3) | copy-start | bytes 4718596
  0.6 5.6 %copy-start = (bf16[192,4096]{1,0:T(8,128)(2,1)S(1)}, bf16[192,4096]{1,0:T(8,128)(2,1)}, u32[]{:S(2)}) copy-start(bf16[192,4096]{1,0:T(8,128)(2,1)} %tok_hbm.3) | copy-start | bytes 4718596
  0.7 5.6 %copy-start.2 = (s32[4]{0:T(128)S(1)}, s32[4]{0:T(128)}, u32[]{:S(2)}) copy-start(s32[4]{0:T(128)} %cap_ref.3) | copy-start | bytes 52
  3.2 44.9 %collective-permute-start = (bf16[208,4096]{1,0:T(8,128)(2,1)}, bf16[208,4096]{1,0:T(8,128)(2,1)}, u32[]{:S(2)}, u32[]{:S(2)}) collective-permute-start(bf16[208,4096]{1,0:T(8,128)(2,1)} %get-tuple-element.26), channel_id=1, source_target_pairs={{0,16},{16,0},{1,17},{17,1},{2,18},{18,2},{3,19},{19,3},{4,20},{20... | collective-permute-start | bytes 5111816 | tf_op jit(solution)/shard_map/ppermute | solution.py:463
  48.1 6.7 %collective-permute-start.1 = (bf16[208,4096]{1,0:T(8,128)(2,1)}, bf16[208,4096]{1,0:T(8,128)(2,1)S(1)}, u32[]{:S(2)}, u32[]{:S(2)}) collective-permute-start(bf16[208,4096]{1,0:T(8,128)(2,1)} %collective-permute-done), channel_id=1, source_target_pairs={{0,1},{1,0},{2,3},{3,2},{4,5},{5,4},{6,7},{7,6},{8,9},{9,8},{10,11... | collective-permute-start | bytes 5111816 | tf_op jit(solution)/shard_map/ppermute | solution.py:470
  48.2 51.2 %all-to-all-start = ((bf16[16,208,256]{2,1,0:T(8,128)(2,1)}), bf16[16,208,256]{2,1,0:T(8,128)(2,1)S(1)}, u32[]{:S(2)}, u32[]{:S(2)}) async-start(bf16[16,208,256]{2,1,0:T(8,128)(2,1)} %get-tuple-element.29), calls=%async_computation | async-start | bytes 3407872 | tf_op jit(solution)/shard_map/all_to_all | solution.py:474
  54.3 33.3 %collective-permute-start.2 = (bf16[3,144,1536]{2,1,0:T(8,128)(2,1)}, bf16[3,144,1536]{2,1,0:T(8,128)(2,1)}, u32[]{:S(2)}, u32[]{:S(2)}) collective-permute-start(bf16[3,144,1536]{2,1,0:T(8,128)(2,1)} %get-tuple-element.40.mine_ref), channel_id=1, source_target_pairs={{0,16},{16,0},{1,17},{17,1},{2,18},{18,2},{3,19},{19,3},{4,20},{20... | collective-permute-start | bytes 3981320 | tf_op jit(solution)/shard_map/ppermute | solution.py:473
  54.8 1.2 %copy-start.3 = (bf16[208,4096]{1,0:T(8,128)(2,1)}, bf16[208,4096]{1,0:T(8,128)(2,1)S(1)}, u32[]{:S(2)}) copy-start(bf16[208,4096]{1,0:T(8,128)(2,1)S(1)} %collective-permute-done.1) | copy-start | bytes 5111812
  87.6 11.9 %copy-start.4 = (s32[192,2]{0,1:T(2,128)S(1)}, s32[192,2]{0,1:T(2,128)}, u32[]{:S(2)}) copy-start(s32[192,2]{0,1:T(2,128)} %param.11) | copy-start | bytes 4612
